TPU v7x, 32 devices: a whole 2x2x4 slice. The times are simulated.
32 devices in a mesh: rep: 2 (over y), seq: 4 (over z), head: 2 (over x), sub: 2 (over core).
Axes of the slice: x: 2, y: 2, z: 4, core: 2. Of those that a mesh axis runs over, the one named last changes fastest.
Arguments:
- key_cache: float32 [8, 32768, 128], P('head', ('rep', 'seq')), parts along dimension 1, may hold values from -40 to 40
- value_cache: bfloat16 [8, 32768, 128], P('head', ('rep', 'seq')), parts along dimension 1, may hold values from -6 to 6
- centroids: float32 [8, 1024, 128], P('head', ('rep', 'sub')), parts along dimension 1, may hold values from -8 to 8
- inv_temp: float32 [8], P('head'), may hold values from 0.015625 to 0.078125
- page_owner: int32 [8, 256, 1], P('head', ('rep', 'seq')), parts along dimension 1, may hold values from 0 to 3; in each aligned block of 32 rows (0 to 31, 32 to 63, ..., all dimensions but the last counted through in order) at most 12 rows name the same one
Outputs:
- clusters: float32 [8, 1024, 128], P('head', ('rep', 'sub')), parts along dimension 1
- moved_keys: bfloat16 [8, 384, 128, 128], P('head', ('rep', 'seq')), parts along dimension 1
- moved_values: bfloat16 [8, 384, 128, 128], P('head', ('rep', 'seq')), parts along dimension 1
- page_ids: int32 [8, 384], P('head', ('rep', 'seq')), parts along dimension 1
There are 2 independent parts, one for each index of `rep`. A program takes and returns all parts, laid end to end along the dimension named above; an argument that names none is the same for every part. Nothing has to cross between parts.
Inputs may be any that keep to these rules, and one draw needn't show every extreme that they name: `page_owner`: among the 32 pages of one head on one index of seq (an aligned block), no owner is named by more than 12 pages, a bound that some block reaches.
All inputs are finite; a program needn't handle non-finite values.
Results may differ from a plain program's by a relative error of at most 0.0075.
Values may be sent and summed in bfloat16 or wider, within the bound.
A program may use at most 128 MiB of HBM per device.

v0:
```python
import jax
import jax.numpy as jnp
from jax import lax
from jax.sharding import PartitionSpec as P

ITERS = 3
PAGE = 128


prior_count = 8.0


def combined_all(value, axis, join):
    pieces = jax.tree.map(lambda part: lax.all_gather(part, axis), value)
    head = jax.tree.map(lambda part: part[0], pieces)
    tail = jax.tree.map(lambda part: part[1:], pieces)
    subtotal, _ = lax.scan(lambda subtotal, section: (join(subtotal, section), None), head, tail)
    return subtotal


def page_slots(page_owner, owner_count, capacity):
    owner_ids = jnp.arange(owner_count, dtype=jnp.int32)
    owner_hits = (page_owner[:, None, :] == owner_ids[None, :, None]).astype(jnp.int32)
    before = jnp.cumsum(owner_hits, axis=2) - owner_hits
    slot_ids = jnp.arange(capacity, dtype=jnp.int32)
    matched = (owner_hits[:, :, None, :] == 1) & (
        before[:, :, None, :] == slot_ids[None, None, :, None]
    )
    page_index = jnp.arange(page_owner.shape[1], dtype=jnp.int32)
    source = jnp.sum(jnp.where(matched, page_index[None, None, None, :], 0), axis=3)
    filled = jnp.any(matched, axis=3)
    head_count = page_owner.shape[0]
    return (
        source.reshape(head_count, owner_count * capacity),
        filled.reshape(head_count, owner_count * capacity),
    )


def take_pages(page_rows, source, filled):
    picked = jax.vmap(lambda head_block, row_index: jnp.take(head_block, row_index, axis=0))(
        page_rows, source
    )
    return jnp.where(filled[:, :, None, None], picked, jnp.zeros((), page_rows.dtype))


def scaled_logits(keys_low, cent_table, inv_temp):
    low_table = cent_table.astype(jnp.bfloat16)
    half_norm = 0.5 * jnp.sum(cent_table * cent_table, axis=2)
    scores = jnp.einsum("htd,hcd->htc", keys_low, low_table, preferred_element_type=jnp.float32)
    return inv_temp[:, None, None] * (scores - half_norm[:, None, :])


def weighted_sums(weights, keys_low):
    key_sums = jnp.einsum("htc,htd->hcd", weights, keys_low, preferred_element_type=jnp.float32)
    resp_mass = jnp.sum(weights, axis=1, dtype=jnp.float32)
    return (key_sums, resp_mass)


def renewed(key_sums, resp_mass, cent_table):
    return (key_sums + prior_count * cent_table) / (resp_mass[:, :, None] + prior_count)


def combine_norms(left_pair, right_pair):
    highest = jnp.maximum(left_pair[0], right_pair[0])
    return (
        highest,
        left_pair[1] * jnp.exp(left_pair[0] - highest)
        + right_pair[1] * jnp.exp(right_pair[0] - highest),
    )


def on_device(key_cache, value_cache, centroids, inv_temp, page_owner):
    keys_low = key_cache.astype(jnp.bfloat16)
    head_count, tok_count, head_width = key_cache.shape
    page_count = tok_count // PAGE
    owner_count = lax.axis_size("seq")
    capacity = max(2, (3 * page_count + 2 * owner_count - 1) // (2 * owner_count))
    source, filled = page_slots(page_owner[:, :, 0], owner_count, capacity)
    page_ids = jnp.where(filled, source + lax.axis_index("seq") * page_count, -1)
    key_pages = take_pages(
        keys_low.reshape(head_count, page_count, PAGE, head_width), source, filled
    )
    value_pages = take_pages(
        value_cache.reshape(head_count, page_count, PAGE, head_width), source, filled
    )
    head_share = head_count // lax.axis_size("sub")
    head_offset = lax.axis_index("sub") * head_share
    key_share = lax.dynamic_slice_in_dim(key_pages, head_offset, head_share, 0)
    value_share = lax.dynamic_slice_in_dim(value_pages, head_offset, head_share, 0)
    id_share = lax.dynamic_slice_in_dim(page_ids, head_offset, head_share, 0)
    got_keys, got_values, got_ids = (
        lax.all_to_all(key_share, "seq", split_axis=1, concat_axis=1, tiled=True),
        lax.all_to_all(value_share, "seq", split_axis=1, concat_axis=1, tiled=True),
        lax.all_to_all(id_share, "seq", split_axis=1, concat_axis=1, tiled=True),
    )
    moved_keys, moved_values, moved_ids = (
        lax.all_gather(got_keys, "sub", axis=0, tiled=True),
        lax.all_gather(got_values, "sub", axis=0, tiled=True),
        lax.all_gather(got_ids, "sub", axis=0, tiled=True),
    )
    cent_table = centroids
    for iteration in range(ITERS):
        logits = scaled_logits(keys_low, cent_table, inv_temp)
        highest = jnp.max(logits, axis=2)
        partial_total = jnp.sum(jnp.exp(logits - highest[:, :, None]), axis=2)
        highest, norm_total = combined_all((highest, partial_total), "sub", combine_norms)
        weights = (jnp.exp(logits - highest[:, :, None]) / norm_total[:, :, None]).astype(
            jnp.bfloat16
        )
        key_sums, resp_mass = weighted_sums(weights, keys_low)
        key_sums, resp_mass = lax.psum((key_sums, resp_mass), "seq")
        cent_table = renewed(key_sums, resp_mass, cent_table)
    return (cent_table, moved_keys, moved_values, moved_ids)


def solution(mesh):
    return jax.shard_map(
        on_device,
        mesh=mesh,
        in_specs=(
            P("head", ("rep", "seq"), None),
            P("head", ("rep", "seq"), None),
            P("head", ("rep", "sub"), None),
            P("head"),
            P("head", ("rep", "seq"), None),
        ),
        out_specs=(
            P("head", ("rep", "sub"), None),
            P("head", ("rep", "seq"), None, None),
            P("head", ("rep", "seq"), None, None),
            P("head", ("rep", "seq")),
        ),
        check_vma=False,
    )
```

profile of v0, /device:TPU:0, one launch (start us, length us, event | category | flops | bytes accessed | tf_op | source)
XLA Modules:
  0.0 361.8 jit_solution(18402554578612585958)
XLA Ops:
  8.0 0.0 all-reduce.4.cloned.1.call-start
  8.0 3.9 %convert_element_type.44 = bf16[4,4096,128]{2,1,0:T(8,128)(2,1)S(1)} convert(f32[4,4096,128]{2,1,0:T(8,128)} %param.7) | non-fusion elementwise | flops 2097152 | bytes 12582912 | tf_op jit(solution)/shard_map/convert_element_type | solution.py:73
  12.0 1.7 multiply_reduce_fusion.2
  13.7 4.2 %fusion.10 = (f32[4,4096]{1,0:T(4,128)}, f32[4,4096,256]{1,2,0:T(8,128)S(1)}) fusion(f32[4,256]{1,0:T(4,128)S(1)} %broadcast_multiply_fusion.2, f32[4]{0:T(128)} %param.10, bf16[4,4096,128]{2,1,0:T(8,128)(2,1)S(1)} %convert_element_type.44, f32[4,256,128]{2,1,0:T(8,128)} %param.9), kind=kOutput, calls=%fused_computation.26 | convolution fusion | flops 1086439424 | bytes 21565456 | tf_op jit(solution)/shard_map/htd,hcd->htc/dot_general | solution.py:49
  17.9 4.6 %exponential_reduce_fusion = f32[4,4096]{1,0:T(4,128)S(1)} fusion(f32[4,4096,256]{1,2,0:T(8,128)S(1)} %get-tuple-element.71, f32[4,4096]{1,0:T(4,128)} %get-tuple-element.70, f32[4,256]{1,0:T(4,128)S(1)} %broadcast_multiply_fusion.2, f32[4]{0:T(128)S(1)} %copy-done.9), kind=kLoop, calls=%fused_computation.24 | loop fusion | flops 16760832 | bytes 16912400 | tf_op jit(solution)/shard_map/reduce_sum | solution.py:105
  22.5 2.0 all-gather.7
  24.6 1.9 all-gather.6
  26.4 0.1 fusion.27
  26.5 5.8 %convert_reduce_fusion.2 = (f32[4,256]{1,0:T(4,128)S(1)}, bf16[4,4096,256]{1,2,0:T(8,128)(2,1)S(1)}) fusion(f32[4,4096]{1,0:T(4,128)S(1)} %get-tuple-element.64, f32[4,4096]{1,0:T(4,128)S(1)} %get-tuple-element.65, f32[4,4096,256]{1,2,0:T(8,128)S(1)} %get-tuple-element.71, f32[4,256]{1,0:T(4,128)S(1)} %broadcast_multiply_fusion.2, f32[4]{0:T(128)S(1)} %copy-done.9), kind=kLoop, calls=%fused_computation.22 | loop fusion | flops 29359104 | bytes 25305104 | tf_op jit(solution)/shard_map/reduce_sum | solution.py:55
  32.3 3.2 fusion.41
  35.5 0.0 all-reduce.4.cloned.1.call-update
  35.6 0.0 all-reduce.6.cloned.1.call-start
  35.6 0.8 reduce_window_sum.11
  36.5 0.9 select_reduce_fusion
  37.4 0.9 fusion.32
  38.3 13.5 %psum.43 = f32[4,256]{1,0:T(4,128)S(1)} all-reduce(f32[4,256]{1,0:T(4,128)S(1)} %get-tuple-element.62), channel_id=1, replica_groups=mesh['rep'=2,'seq'=4,'head'=2,'sub'=2] {'seq'}, use_global_device_ids=true, to_apply=%region_5.6 | all-reduce | flops 1024 | bytes 8192 | tf_op jit(solution)/shard_map/psum | solution.py:111
  51.8 0.1 copy.29
  51.9 0.1 reshape.173
  52.0 0.1 copy.28
  52.1 0.1 broadcast_in_dim.43
  52.2 0.1 reshape.255
  52.3 11.6 %gather_fusion = bf16[192,128,128]{2,1,0:T(8,128)(2,1)} fusion(bf16[4,32,128,128]{3,2,1,0:T(8,128)(2,1)} %bitcast.134, s32[192]{0:T(256)S(1)} %reshape.255), kind=kCustom, calls=%fused_computation.clone | custom fusion | bytes 12584448 | tf_op jit(solution)/shard_map/vmap(jit(_take))/gather | solution.py:40
  63.9 11.7 %gather_fusion.1 = bf16[192,128,128]{2,1,0:T(8,128)(2,1)} fusion(bf16[4,32,128,128]{3,2,1,0:T(8,128)(2,1)} %bitcast.137, s32[192]{0:T(256)S(1)} %reshape.255), kind=kCustom, calls=%fused_computation.1.clone | custom fusion | bytes 12584448 | tf_op jit(solution)/shard_map/vmap(jit(_take))/gather | solution.py:40
  75.6 1.2 all-reduce.4.cloned.1.call-done
  76.8 1.4 multiply_reduce_fusion.1
  78.3 4.4 %bitcast_reduce_fusion.1 = (f32[4,4096]{1,0:T(4,128)S(1)}, f32[4,256,4096]{2,1,0:T(8,128)S(1)}) fusion(f32[4,256]{1,0:T(4,128)S(1)} %broadcast_multiply_fusion.1, f32[4]{0:T(128)S(1)} %copy-done.9, bf16[4,4096,128]{2,1,0:T(8,128)(2,1)} %copy-done, f32[4,256,128]{2,1,0:T(8,128)S(1)} %get-tuple-element.61), kind=kOutput, calls=%fused_computation.12 | convolution fusion | flops 1086439424 | bytes 21565456 | tf_op jit(solution)/shard_map/htd,hcd->htc/dot_general | solution.py:49
  82.7 3.7 %fusion.9 = f32[4,4096]{1,0:T(4,128)S(1)} fusion(f32[4,256,4096]{2,1,0:T(8,128)S(1)} %get-tuple-element.73, f32[4,4096]{1,0:T(4,128)S(1)} %get-tuple-element.72, f32[4,256]{1,0:T(4,128)S(1)} %broadcast_multiply_fusion.1, f32[4]{0:T(128)S(1)} %copy-done.9), kind=kLoop, calls=%fused_computation.17 | loop fusion | flops 16760832 | bytes 16912400 | tf_op jit(solution)/shard_map/reduce_sum | solution.py:105
  86.4 2.0 all-gather.9
  88.4 2.1 all-gather.8
  90.5 0.1 fusion.24
  90.6 7.2 %convert_reduce_fusion.1 = (f32[4,256]{1,0:T(4,128)S(1)}, bf16[4,4096,256]{1,2,0:T(8,128)(2,1)}) fusion(f32[4,4096]{1,0:T(4,128)S(1)} %get-tuple-element.53, f32[4,4096]{1,0:T(4,128)S(1)} %get-tuple-element.54, f32[4,256,4096]{2,1,0:T(8,128)S(1)} %get-tuple-element.73, f32[4,256]{1,0:T(4,128)S(1)} %broadcast_multiply_fusion.1, f32[4]{0:T(128)S(1)} %copy-done.9), kind=kLoop, calls=%fused_computation.20 | loop fusion | flops 29359104 | bytes 25305104 | tf_op jit(solution)/shard_map/reduce_sum | solution.py:55
  97.8 6.6 %fusion.42 = f32[4,256,128]{2,1,0:T(8,128)} fusion(bf16[4,4096,256]{1,2,0:T(8,128)(2,1)} %get-tuple-element.52, bf16[4,4096,128]{2,1,0:T(8,128)(2,1)S(1)} %copy-done.1), kind=kOutput, calls=%fused_computation.89 | convolution fusion | flops 1073741824 | bytes 13107200 | tf_op jit(solution)/shard_map/htc,htd->hcd/dot_general | solution.py:54
  104.4 0.0 all-reduce.6.cloned.1.call-update
  104.4 4.5 %fusion.11 = (bf16[2,48,128,128]{3,2,1,0:T(8,128)(2,1)}, bf16[2,48,128,128]{3,2,1,0:T(8,128)(2,1)S(1)}) fusion(bf16[4,48,128,128]{3,2,1,0:T(8,128)(2,1)} %bitcast.136, s32[]{:T(128)S(6)} %select_n.29, pred[2,48]{1,0:T(4,128)(4,1)S(1)} %get-tuple-element.77, pred[2,48]{1,0:T(4,128)(4,1)S(1)} %get-tuple-element.76, bf16[4,48,128,128]{3,2,1,0:T(8,128)(2,1)} %bitcast.135), kind=kLoop, calls=%fused_computation.28 | loop fusion | flops 6291456 | bytes 12583108 | tf_op jit(solution)/shard_map/jit(_where)/select_n | solution.py:43
  108.9 2.1 copy.30
  111.0 3.7 %all-to-all-start = ((bf16[2,48,128,128]{3,2,0,1:T(8,128)(2,1)}), bf16[2,48,128,128]{3,2,0,1:T(8,128)(2,1)S(1)}, u32[]{:S(2)}, u32[]{:S(2)}) async-start(bf16[2,48,128,128]{3,2,0,1:T(8,128)(2,1)} %copy.30), calls=%async_computation | async-start | bytes 6291456 | tf_op jit(solution)/shard_map/all_to_all | solution.py:92
  114.7 0.0 all-reduce.8.cloned.1.call-start
  114.8 69.9 %psum.45 = f32[4,256]{1,0:T(4,128)S(1)} all-reduce(f32[4,256]{1,0:T(4,128)S(1)} %get-tuple-element.51), channel_id=1, replica_groups=mesh['rep'=2,'seq'=4,'head'=2,'sub'=2] {'seq'}, use_global_device_ids=true, to_apply=%region_11.12 | all-reduce | flops 1024 | bytes 8192 | tf_op jit(solution)/shard_map/psum | solution.py:111
  184.6 1.6 multiply_reduce_fusion
  186.2 4.4 %bitcast_reduce_fusion = (f32[4,4096]{1,0:T(4,128)S(1)}, f32[4,256,4096]{2,1,0:T(8,128)S(1)}) fusion(f32[4,256]{1,0:T(4,128)S(1)} %broadcast_multiply_fusion, f32[4]{0:T(128)S(1)} %copy-done.9, bf16[4,4096,128]{2,1,0:T(8,128)(2,1)} %copy-done, f32[4,256,128]{2,1,0:T(8,128)S(1)} %get-tuple-element.50), kind=kOutput, calls=%fused_computation.4 | convolution fusion | flops 1086439424 | bytes 21565456 | tf_op jit(solution)/shard_map/htd,hcd->htc/dot_general | solution.py:49
  190.6 3.7 %fusion.4 = f32[4,4096]{1,0:T(4,128)S(1)} fusion(f32[4,256,4096]{2,1,0:T(8,128)S(1)} %get-tuple-element.75, f32[4,4096]{1,0:T(4,128)S(1)} %get-tuple-element.74, f32[4,256]{1,0:T(4,128)S(1)} %broadcast_multiply_fusion, f32[4]{0:T(128)S(1)} %copy-done.9), kind=kLoop, calls=%fused_computation.9 | loop fusion | flops 16760832 | bytes 16912400 | tf_op jit(solution)/shard_map/reduce_sum | solution.py:105
  194.4 2.0 all-gather.11
  196.4 1.9 all-gather.10
  198.3 0.1 fusion.21
  198.3 7.1 %convert_reduce_fusion = (f32[4,256]{1,0:T(4,128)S(1)}, bf16[4,4096,256]{1,2,0:T(8,128)(2,1)}) fusion(f32[4,4096]{1,0:T(4,128)S(1)} %get-tuple-element.42, f32[4,4096]{1,0:T(4,128)S(1)} %get-tuple-element.43, f32[4,256,4096]{2,1,0:T(8,128)S(1)} %get-tuple-element.75, f32[4,256]{1,0:T(4,128)S(1)} %broadcast_multiply_fusion, f32[4]{0:T(128)S(1)} %copy-done.9), kind=kLoop, calls=%fused_computation.18 | loop fusion | flops 29359104 | bytes 25305104 | tf_op jit(solution)/shard_map/reduce_sum | solution.py:55
  205.4 6.6 %fusion.43 = f32[4,256,128]{2,1,0:T(8,128)} fusion(bf16[4,4096,256]{1,2,0:T(8,128)(2,1)} %get-tuple-element.41, bf16[4,4096,128]{2,1,0:T(8,128)(2,1)S(1)} %copy-done.2), kind=kOutput, calls=%fused_computation.90 | convolution fusion | flops 1073741824 | bytes 13107200 | tf_op jit(solution)/shard_map/htc,htd->hcd/dot_general | solution.py:54
  212.0 0.0 all-reduce.8.cloned.1.call-update
  212.1 0.0 all-gather.16.cloned.1.call-start
  212.1 1.9 copy.31
  214.0 0.0 all-gather.16.cloned.1.call-update
  214.0 0.0 all-gather.18.cloned.1.call-start
  214.1 2.3 copy.32
  216.4 103.7 %all_to_all.22 = bf16[2,48,128,128]{3,2,0,1:T(8,128)(2,1)S(1)} all-to-all(bf16[2,48,128,128]{3,2,0,1:T(8,128)(2,1)S(1)} %copy.32), channel_id=1, replica_groups=mesh['rep'=2,'seq'=4,'head'=2,'sub'=2] {'seq'}, dimensions={1} | all-to-all | bytes 6291456 | tf_op jit(solution)/shard_map/all_to_all | solution.py:93
  320.1 2.1 copy.33
  322.2 0.0 all-gather.18.cloned.1.call-update
  322.3 0.1 all_to_all.16
  322.4 7.9 %all_to_all.23 = s32[2,4,12]{2,0,1:T(2,128)S(1)} all-to-all(s32[2,4,12]{2,0,1:T(2,128)S(1)} %copy.34), channel_id=1, replica_groups=mesh['rep'=2,'seq'=4,'head'=2,'sub'=2] {'seq'}, dimensions={1} | all-to-all | bytes 768 | tf_op jit(solution)/shard_map/all_to_all | solution.py:94
  330.3 0.1 reshape.239
  330.4 1.8 all-gather.12
  332.1 8.9 %psum.47 = f32[4,256]{1,0:T(4,128)S(1)} all-reduce(f32[4,256]{1,0:T(4,128)S(1)} %get-tuple-element.40), channel_id=1, replica_groups=mesh['rep'=2,'seq'=4,'head'=2,'sub'=2] {'seq'}, use_global_device_ids=true, to_apply=%region_17.18 | all-reduce | flops 1024 | bytes 8192 | tf_op jit(solution)/shard_map/psum | solution.py:111
  341.1 2.0 add_divide_fusion
  343.1 8.3 %copy.42 = bf16[4,48,128,128]{3,2,1,0:T(8,128)(2,1)} copy(bf16[4,48,128,128]{3,2,1,0:T(8,128)(2,1)} %all-gather.16.cloned.1.call-done) | data formatting | bytes 12582912
  351.4 2.7 copy.43
  354.1 0.6 copy.44
  (42 shorter events, 0.2 us)
Async XLA Ops:
  8.0 68.8 %all-reduce.4.cloned.1.call-start = ((), (), s32[]{:S(2)}) async-start(), calls=%async_computation.3 | async-start | bytes 1048576 | tf_op jit(solution)/shard_map/psum | solution.py:111
  12.0 20.4 %copy-start = (bf16[4,4096,128]{2,1,0:T(8,128)(2,1)}, bf16[4,4096,128]{2,1,0:T(8,128)(2,1)S(1)}, u32[]{:S(2)}) copy-start(bf16[4,4096,128]{2,1,0:T(8,128)(2,1)S(1)} %convert_element_type.44) | copy-start | bytes 12582916
  12.0 6.0 %copy-start.9 = (f32[4]{0:T(128)S(1)}, f32[4]{0:T(128)}, u32[]{:S(2)}) copy-start(f32[4]{0:T(128)} %param.10) | copy-start | bytes 52
  17.9 6.6 %copy-start.8 = (f32[4,4096]{1,0:T(4,128)S(1)}, f32[4,4096]{1,0:T(4,128)}, u32[]{:S(2)}) copy-start(f32[4,4096]{1,0:T(4,128)} %get-tuple-element.70) | copy-start | bytes 196612
  26.5 9.1 %copy-start.10 = (s32[4,32,1]{1,2,0:T(1,128)S(1)}, s32[4,32,1]{1,2,0:T(1,128)}, u32[]{:S(2)}) copy-start(s32[4,32,1]{1,2,0:T(1,128)} %param.11) | copy-start | bytes 1540
  32.3 44.5 %copy-start.6 = (f32[4,256,128]{2,1,0:T(8,128)S(1)}, f32[4,256,128]{2,1,0:T(8,128)}, u32[]{:S(2)}) copy-start(f32[4,256,128]{2,1,0:T(8,128)} %param.9) | copy-start | bytes 1572868
  35.6 149.1 %all-reduce.6.cloned.1.call-start = ((), (), s32[]{:S(2)}) async-start(), calls=%async_computation.4 | async-start | bytes 1048576 | tf_op jit(solution)/shard_map/psum | solution.py:111
  78.2 8.1 %copy-start.5 = (f32[4,256,128]{2,1,0:T(8,128)}, f32[4,256,128]{2,1,0:T(8,128)S(1)}, u32[]{:S(2)}) copy-start(f32[4,256,128]{2,1,0:T(8,128)S(1)} %get-tuple-element.61) | copy-start | bytes 1572868
  86.4 11.4 %copy-start.1 = (bf16[4,4096,128]{2,1,0:T(8,128)(2,1)S(1)}, bf16[4,4096,128]{2,1,0:T(8,128)(2,1)}, u32[]{:S(2)}) copy-start(bf16[4,4096,128]{2,1,0:T(8,128)(2,1)} %copy-done) | copy-start | bytes 12582916
  111.0 101.1 %all-to-all-start = ((bf16[2,48,128,128]{3,2,0,1:T(8,128)(2,1)}), bf16[2,48,128,128]{3,2,0,1:T(8,128)(2,1)S(1)}, u32[]{:S(2)}, u32[]{:S(2)}) async-start(bf16[2,48,128,128]{3,2,0,1:T(8,128)(2,1)} %copy.30), calls=%async_computation | async-start | bytes 6291456 | tf_op jit(solution)/shard_map/all_to_all | solution.py:92
  114.7 226.4 %all-reduce.8.cloned.1.call-start = ((), (), s32[]{:S(2)}) async-start(), calls=%async_computation.5 | async-start | bytes 1048576 | tf_op jit(solution)/shard_map/psum | solution.py:111
  186.2 8.1 %copy-start.3 = (f32[4,256,128]{2,1,0:T(8,128)}, f32[4,256,128]{2,1,0:T(8,128)S(1)}, u32[]{:S(2)}) copy-start(f32[4,256,128]{2,1,0:T(8,128)S(1)} %get-tuple-element.50) | copy-start | bytes 1572868
  194.4 11.1 %copy-start.2 = (bf16[4,4096,128]{2,1,0:T(8,128)(2,1)S(1)}, bf16[4,4096,128]{2,1,0:T(8,128)(2,1)}, u32[]{:S(2)}) copy-start(bf16[4,4096,128]{2,1,0:T(8,128)(2,1)} %copy-done) | copy-start | bytes 12582916
  212.1 131.1 %all-gather.16.cloned.1.call-start = ((), (), s32[]{:S(2)}) async-start(), calls=%async_computation.6 | async-start | bytes 9437184 | tf_op jit(solution)/shard_map/all_gather | solution.py:97
  214.0 127.1 %copy-start.4 = (f32[4,256,128]{2,1,0:T(8,128)S(1)}, f32[4,256,128]{2,1,0:T(8,128)}, u32[]{:S(2)}) copy-start(f32[4,256,128]{2,1,0:T(8,128)} %copy-done.3) | copy-start | bytes 1572868
  214.0 129.1 %all-gather.18.cloned.1.call-start = ((), (), s32[]{:S(2)}) async-start(), calls=%async_computation.7 | async-start | bytes 9437184 | tf_op jit(solution)/shard_map/all_gather | solution.py:98
  343.1 8.3 %copy-start.7 = (bf16[4,48,128,128]{3,2,1,0:T(8,128)(2,1)S(1)}, bf16[4,48,128,128]{3,2,1,0:T(8,128)(2,1)}, u32[]{:S(2)}) copy-start(bf16[4,48,128,128]{3,2,1,0:T(8,128)(2,1)} %all-gather.18.cloned.1.call-done) | copy-start | bytes 18874372
Sparse Core Ops, SparseCore 0:
  35.7 41.0 all-reduce.3
  104.5 76.6 all-reduce.5
  212.2 73.5 all-reduce.7
Sparse Core Ops, SparseCore 1:
  214.7 31.5 all-gather.15
  322.3 15.4 all-gather.17
where the time goes:
time: 363 us; the launch traced here: 362 us
  blocking collectives  218 us (60%)
  other arithmetic  50.2 us (14%)
  local copies, waits for them, and re-layouts  44 us (12%)
  matrix products  29.4 us (8%)
  between operations  15.5 us (4%)
  starting transfers between devices  3.91 us (1%)
    all_to_all x1, blocking collectives, on_device(): lax.all_to_all(value_share, 'seq', split_axis=1, concat_axis=1, tiled=True)  104 us
    psum x3, blocking collectives, on_device(): key_sums, resp_mass = lax.psum((key_sums, resp_mass), 'seq')  92.2 us
    gather x3, local copies, waits for them, and re-layouts, take_pages(): jnp.take(head_block, row_index, axis=0)  23.4 us
    reduce_sum x3, other arithmetic, weighted_sums(): resp_mass = jnp.sum(weights, axis=1, dtype=jnp.float32)  20.1 us
    dot_general x3, matrix products, weighted_sums(): jnp.einsum('htc,htd->hcd', weights, keys_low, preferred_element_type=jnp....  16.4 us
    dot_general x3, matrix products, scaled_logits(): jnp.einsum('htd,hcd->htc', keys_low, low_table, preferred_element_type=jn...  13 us
    reduce_sum x3, other arithmetic, on_device(): partial_total = jnp.sum(jnp.exp(logits - highest[:, :, None]), axis=2)  12 us
    all_gather x6, blocking collectives, combined_all(): pieces = jax.tree.map(lambda part: lax.all_gather(part, axis), value)  11.9 us
  transfers between devices with their start and end apart: 6, of which 1 were waited for; matrix products, arithmetic and copies ran while one was open for 18% of the time, Pallas kernels for 0%

commit v1 on v0

v1 whole, which is shorter than its diff:
```python
import functools
import math

import jax
import jax.numpy as jnp
from jax import lax
from jax.experimental import pallas as pl
from jax.experimental.pallas import tpu as pltpu
from jax.sharding import PartitionSpec as P

ITERS = 3
PAGE = 128
LANES = 128
TILE = 512
MESH = pl.DeviceIdType.MESH

prior_count = 8.0


def page_slots(page_owner, owner_count, capacity):
    pages = page_owner.shape[1]
    index = jnp.arange(pages, dtype=jnp.int32)
    same = page_owner[:, :, None] == page_owner[:, None, :]
    rank = jnp.sum(jnp.where(same & (index[None, :] < index[:, None]), 1, 0), axis=2)
    place = page_owner * capacity + rank
    slot_ids = jnp.arange(owner_count * capacity, dtype=jnp.int32)
    hits = place[:, None, :] == slot_ids[None, :, None]
    return jnp.sum(jnp.where(hits, index + 1, 0), axis=2) - 1


def gather_kernel(share, owners, capacity, slots_ref, first_ref, key_ref, value_ref,
                  low_ref, send_key_ref, send_value_ref):
    base = (first_ref[0] + pl.program_id(0)) * (owners * capacity)
    low_ref[0] = key_ref[0].astype(jnp.bfloat16)
    for owner in range(owners):
        for slot in range(capacity):
            page = slots_ref[base + owner * capacity + slot]
            filled = page >= 0
            page = jnp.maximum(page, 0)
            rows = pl.ds(pl.multiple_of(page * PAGE, PAGE), PAGE)

            @pl.when(filled)
            def _():
                send_key_ref[owner, 0, slot] = key_ref[0, rows, :].astype(jnp.bfloat16)
                send_value_ref[owner, 0, slot] = value_ref[0, rows, :]

            @pl.when(jnp.logical_not(filled))
            def _():
                send_key_ref[owner, 0, slot] = jnp.zeros((PAGE, LANES), jnp.bfloat16)
                send_value_ref[owner, 0, slot] = jnp.zeros((PAGE, LANES), jnp.bfloat16)


def partner(me, step, owners):
    out = 0
    bit = 1
    while bit < owners:
        own = lax.rem(lax.div(me, bit), 2)
        out = out + lax.rem(own + (1 if step & bit else 0), 2) * bit
        bit *= 2
    return out


def cluster_kernel(owners, share, capacity, low_ref, cent_ref, rate_ref, ids_ref,
                   send_key_ref, send_value_ref,
                   clusters_ref, moved_key_ref, moved_value_ref, moved_ids_ref,
                   keys_aug, table, table_aug, acc, part, part_in, mass, mass_in, total_rep,
                   ids_in, fin,
                   page_sems, fwd_sems, own_sems, own_fwd_sems, sum_sems, mass_sems, table_sems,
                   ids_sems, cent_sems, fin_sems):
    me = lax.axis_index("seq")
    sub = lax.axis_index("sub")
    sib = 1 - sub
    cents = table.shape[2]
    half = cent_ref.shape[1]
    quarter = cents // owners
    tokens = low_ref.shape[1]
    partners = [partner(me, step, owners) for step in range(1, owners)]

    barrier = pltpu.get_barrier_semaphore()
    for q in partners:
        pl.semaphore_signal(barrier, inc=1, device_id={"seq": q}, device_id_type=MESH)
    pl.semaphore_signal(barrier, inc=1, device_id={"sub": sib}, device_id_type=MESH)
    pl.semaphore_wait(barrier, owners)

    def remote(src, dst, sems, at, device):
        return pltpu.make_async_remote_copy(
            src_ref=src, dst_ref=dst, send_sem=sems.at[(0, *at)], recv_sem=sems.at[(1, *at)],
            device_id=device, device_id_type=MESH,
        )

    waits = []
    first_head = sub * share
    cent_copy = remote(cent_ref.at[pl.ds(sib * share, share)],
                       table.at[0, :, pl.ds(pl.multiple_of(sub * half, half), half), :],
                       cent_sems, (), {"sub": sib})
    cent_copy.start()
    ids_copies = []
    for i, q in enumerate(partners):
        c = remote(ids_ref.at[q], ids_in.at[me], ids_sems, (i,), {"seq": q})
        c.start()
        ids_copies.append(c)

    arrays = ((send_key_ref, moved_key_ref), (send_value_ref, moved_value_ref))
    my_slots = pl.ds(me * capacity, capacity)
    own_copies = []
    for a, (src, dst) in enumerate(arrays):
        for h in range(share):
            c = pltpu.make_async_copy(src.at[me, h], dst.at[first_head + h, my_slots],
                                      own_sems.at[a, h])
            c.start()
            f = remote(src.at[me, h], dst.at[first_head + h, my_slots], own_fwd_sems, (a, h),
                       {"sub": sib})
            f.start()
            own_copies += [(c, f)]
    order = []
    far = [i for i in range(owners - 1) if i + 1 >= owners // 2]
    near = [i for i in range(owners - 1) if i + 1 < owners // 2]
    far_list = [(i, a, h) for i in reversed(far) for a in range(2) for h in range(share)]
    near_list = [(i, a, h) for i in reversed(near) for a in range(2) for h in range(share)]
    while far_list or near_list:
        take = 2 if near_list else len(far_list)
        order += far_list[:take]
        far_list = far_list[take:]
        order += near_list[:1]
        near_list = near_list[1:]
    page_copies = []
    for i, a, h in order:
        src, dst = arrays[a]
        q = partners[i]
        page_copies.append((
            remote(src.at[q, h], dst.at[first_head + h, my_slots], page_sems, (i, a, h), {"seq": q}),
            remote(dst.at[first_head + h, pl.ds(q * capacity, capacity)],
                   dst.at[first_head + h, pl.ds(q * capacity, capacity)],
                   fwd_sems, (i, a, h), {"sub": sib}),
        ))
    phases = 2 * ITERS
    started = [0]

    def start_pages(upto):
        while started[0] < min(upto, len(page_copies)):
            page_copies[started[0]][0].start()
            started[0] += 1

    step_pages = max(1, len(page_copies) // (2 * phases))
    start_pages(2 * step_pages)

    for h in range(share):
        keys_aug[h, :, :LANES] = low_ref[h]
        keys_aug[h, :, LANES:] = jnp.ones((tokens, LANES), jnp.bfloat16)
        table[0, h, pl.ds(pl.multiple_of(sub * half, half), half), :] = cent_ref[first_head + h]
    cent_copy.wait()

    lane = lax.broadcasted_iota(jnp.int32, (cents, LANES), 1)
    eye = (lax.broadcasted_iota(jnp.int32, (LANES, LANES), 0)
           == lax.broadcasted_iota(jnp.int32, (LANES, LANES), 1))
    blocks = cents // LANES
    for it in range(ITERS):
        for h in range(share):
            rows = table[it, h]
            norm = jnp.broadcast_to(-0.5 * jnp.sum(rows * rows, axis=1, keepdims=True), rows.shape)
            high = norm.astype(jnp.bfloat16).astype(jnp.float32)
            rest = norm - high
            mid = rest.astype(jnp.bfloat16).astype(jnp.float32)
            low = rest - mid
            extra = jnp.where(lane == 0, high, jnp.where(lane == 1, mid, jnp.where(lane == 2, low, 0.0)))
            table_aug[h, :, :LANES] = rows.astype(jnp.bfloat16)
            table_aug[h, :, LANES:] = extra.astype(jnp.bfloat16)
            acc[h] = jnp.zeros((cents, 2 * LANES), jnp.float32)
            rate = rate_ref[h, 0:1, 0:1] * (1.0 / math.log(2.0))

            def sweep(i, carry, h=h, rate=rate):
                k = keys_aug[h, pl.ds(pl.multiple_of(i * TILE, TILE), TILE), :]
                s = lax.dot_general(table_aug[h], k, (((1,), (1,)), ((), ())),
                                    preferred_element_type=jnp.float32)
                top = jnp.max(s, axis=0, keepdims=True)
                p = jnp.exp2((s - top) * rate)
                w = (p * (1.0 / jnp.sum(p, axis=0, keepdims=True))).astype(jnp.bfloat16)
                acc[h] += jnp.dot(w, k, preferred_element_type=jnp.float32)
                return carry

            lax.fori_loop(0, tokens // TILE, sweep, 0)
        for h in range(share):
            part[it, h] = acc[h, :, :LANES].astype(jnp.bfloat16)
            for b in range(blocks):
                rep = acc[h, b * LANES:(b + 1) * LANES, LANES:]
                mass[it, h * blocks + b:h * blocks + b + 1, :] = jnp.sum(
                    jnp.where(eye, rep, 0.0), axis=0, keepdims=True)
        copies = []
        for i, q in enumerate(partners):
            c = remote(part.at[it, :, pl.ds(pl.multiple_of(q * quarter, quarter), quarter), :],
                       part_in.at[it, i], sum_sems, (it, i), {"seq": q})
            m = remote(mass.at[it], mass_in.at[it, i], mass_sems, (it, i), {"seq": q})
            c.start()
            m.start()
            copies += [c, m]
        start_pages((3 + 2 * it) * step_pages)
        for c in copies:
            c.wait()
        masses = mass[it]
        for i in range(owners - 1):
            masses = masses + mass_in[it, i]
        mine = pl.ds(pl.multiple_of(me * quarter, quarter), quarter)
        for h in range(share):
            for b in range(blocks):
                row = masses[h * blocks + b:h * blocks + b + 1, :]
                total_rep[b * LANES:(b + 1) * LANES, :] = jnp.broadcast_to(
                    jnp.sum(jnp.where(eye, row, 0.0), axis=1, keepdims=True), (LANES, LANES))
            sums = acc[h, mine, :LANES]
            for i in range(owners - 1):
                sums = sums + part_in[it, i, h].astype(jnp.float32)
            table[it + 1, h, mine, :] = (sums + prior_count * table[it, h, mine, :]) / (
                total_rep[mine, :] + prior_count)
        copies = []
        for i, q in enumerate(partners):
            c = remote(table.at[it + 1, :, mine, :], table.at[it + 1, :, mine, :],
                       table_sems, (it, i), {"seq": q})
            c.start()
            copies.append(c)
        start_pages((4 + 2 * it) * step_pages)
        for c in copies:
            c.wait()

    start_pages(len(page_copies))
    fin_copy = remote(table.at[ITERS, :, pl.ds(pl.multiple_of(sib * half, half), half), :], fin,
                      fin_sems, (), {"sub": sib})
    fin_copy.start()
    for h in range(share):
        clusters_ref[first_head + h] = table[ITERS, h, pl.ds(pl.multiple_of(sub * half, half), half), :]
    fin_copy.wait()
    for h in range(share):
        clusters_ref[sib * share + h] = fin[h]
    for c in ids_copies:
        c.wait()
    ids_in[me] = ids_ref[me]
    moved_ids_ref[...] = ids_in[...]
    for c, f in own_copies:
        c.wait()
        f.wait()
    for c, f in page_copies:
        c.wait_recv()
        f.start()
    for c, f in page_copies:
        c.wait_send()
        f.wait()


def on_device(key_cache, value_cache, centroids, inv_temp, page_owner):
    heads, tokens, width = key_cache.shape
    pages = tokens // PAGE
    owners = lax.axis_size("seq")
    capacity = max(2, (3 * pages + 2 * owners - 1) // (2 * owners))
    share = heads // lax.axis_size("sub")
    half = centroids.shape[1]
    cents = half * lax.axis_size("sub")
    quarter = cents // owners
    first = lax.axis_index("sub") * share
    slots = page_slots(page_owner[:, :, 0], owners, capacity)
    ids = jnp.where(slots >= 0, slots + lax.axis_index("seq") * pages, -1)
    ids = jnp.transpose(ids.reshape(heads, owners, capacity), (1, 0, 2))
    ids = jnp.pad(ids, ((0, 0), (0, 8 - heads), (0, LANES - capacity)))

    low = jax.ShapeDtypeStruct((share, tokens, width), jnp.bfloat16)
    sent = jax.ShapeDtypeStruct((owners, share, capacity, PAGE, width), jnp.bfloat16)
    keys_low, send_keys, send_values = pl.pallas_call(
        functools.partial(gather_kernel, share, owners, capacity),
        out_shape=(low, sent, sent),
        grid_spec=pltpu.PrefetchScalarGridSpec(
            num_scalar_prefetch=2,
            grid=(share,),
            in_specs=[
                pl.BlockSpec((1, tokens, width), lambda h, s, f: (f[0] + h, 0, 0)),
                pl.BlockSpec((1, tokens, width), lambda h, s, f: (f[0] + h, 0, 0)),
            ],
            out_specs=[
                pl.BlockSpec((1, tokens, width), lambda h, s, f: (h, 0, 0)),
                pl.BlockSpec((owners, 1, capacity, PAGE, width), lambda h, s, f: (0, h, 0, 0, 0)),
                pl.BlockSpec((owners, 1, capacity, PAGE, width), lambda h, s, f: (0, h, 0, 0, 0)),
            ],
        ),
        compiler_params=pltpu.CompilerParams(vmem_limit_bytes=40 * 2**20),
        name="gather_pages",
    )(slots.reshape(-1), first.reshape(1), key_cache, value_cache)

    rates = jnp.broadcast_to(
        lax.dynamic_slice_in_dim(inv_temp, first, share, 0)[:, None, None], (share, 8, LANES))
    moved = jax.ShapeDtypeStruct((heads, owners * capacity, PAGE, width), jnp.bfloat16)
    vmem = pl.BlockSpec(memory_space=pltpu.VMEM)
    anyspace = pl.BlockSpec(memory_space=pl.ANY)
    dma = pltpu.SemaphoreType.DMA
    rest = owners - 1
    clusters, moved_keys, moved_values, moved_ids = pl.pallas_call(
        functools.partial(cluster_kernel, owners, share, capacity),
        out_shape=(
            jax.ShapeDtypeStruct(centroids.shape, jnp.float32), moved, moved,
            jax.ShapeDtypeStruct((owners, 8, LANES), jnp.int32),
        ),
        in_specs=[vmem, vmem, vmem, vmem, anyspace, anyspace],
        out_specs=[vmem, anyspace, anyspace, vmem],
        scratch_shapes=[
            pltpu.VMEM((share, tokens, 2 * LANES), jnp.bfloat16),
            pltpu.VMEM((ITERS + 1, share, cents, width), jnp.float32),
            pltpu.VMEM((share, cents, 2 * LANES), jnp.bfloat16),
            pltpu.VMEM((share, cents, 2 * LANES), jnp.float32),
            pltpu.VMEM((ITERS, share, cents, width), jnp.bfloat16),
            pltpu.VMEM((ITERS, rest, share, quarter, width), jnp.bfloat16),
            pltpu.VMEM((ITERS, 8, LANES), jnp.float32),
            pltpu.VMEM((ITERS, rest, 8, LANES), jnp.float32),
            pltpu.VMEM((cents, LANES), jnp.float32),
            pltpu.VMEM((owners, 8, LANES), jnp.int32),
            pltpu.VMEM((share, half, width), jnp.float32),
            dma((2, rest, 2, share)),
            dma((2, rest, 2, share)),
            dma((2, share)),
            dma((2, 2, share)),
            dma((2, ITERS, rest)),
            dma((2, ITERS, rest)),
            dma((2, ITERS, rest)),
            dma((2, rest)),
            dma((2,)),
            dma((2,)),
        ],
        compiler_params=pltpu.CompilerParams(
            collective_id=0, has_side_effects=True, vmem_limit_bytes=48 * 2**20),
        name="cluster_and_move",
    )(keys_low, centroids, rates, ids, send_keys, send_values)
    moved_ids = jnp.transpose(moved_ids[:, :heads, :capacity], (1, 0, 2)).reshape(heads, owners * capacity)
    return clusters, moved_keys, moved_values, moved_ids


def solution(mesh):
    return jax.shard_map(
        on_device,
        mesh=mesh,
        in_specs=(
            P("head", ("rep", "seq"), None),
            P("head", ("rep", "seq"), None),
            P("head", ("rep", "sub"), None),
            P("head"),
            P("head", ("rep", "seq"), None),
        ),
        out_specs=(
            P("head", ("rep", "sub"), None),
            P("head", ("rep", "seq"), None, None),
            P("head", ("rep", "seq"), None, None),
            P("head", ("rep", "seq")),
        ),
        check_vma=False,
    )
```

time: 363 us -> 239 us (0.66)
  blocking collectives: 218 us -> 0 us
  Pallas kernels: 0 us -> 217 us
  other arithmetic: 50.2 us -> 1.78 us
  matrix products: 29.4 us -> 0 us
  local copies, waits for them, and re-layouts: 44 us -> 19.4 us
  between operations: 15.5 us -> 0.7 us
  starting transfers between devices: 3.91 us -> 0 us
    pallas_call x0 -> x2, Pallas kernels: none -> 217 us  [the longest x1 213 us: on_device(): pl.pallas_call(functools.partial(cluster_kernel, owners, share, capacity)...]
    all_to_all x2 -> x0, blocking collectives: 112 us -> none  [the longest x1 104 us: on_device(): lax.all_to_all(value_share, 'seq', split_axis=1, concat_axis=1, tiled=True)]
    psum x3 -> x0, blocking collectives: 92.2 us -> none  [on_device(): key_sums, resp_mass = lax.psum((key_sums, resp_mass), 'seq')]
    reduce_sum x10 -> x2, other arithmetic: 37.7 us -> 1.07 us  [the longest x1 0.97 us: page_slots(): jnp.sum(jnp.where(same & (index[None, :] < index[:, None]), 1, 0), axis=2)]
    dot_general x6 -> x0, matrix products: 29.4 us -> none  [the longest x3 16.4 us: weighted_sums(): jnp.einsum('htc,htd->hcd', weights, keys_low, preferred_element_type=jnp....]
    gather x3 -> x0, local copies, waits for them, and re-layouts: 23.4 us -> none  [take_pages(): jnp.take(head_block, row_index, axis=0)]
    all_gather x7 -> x0, blocking collectives: 13.7 us -> none  [the longest x6 11.9 us: combined_all(): pieces = jax.tree.map(lambda part: lax.all_gather(part, axis), value)]
    unnamed x26 -> x15, local copies, waits for them, and re-layouts: 11.7 us -> 17.7 us
  transfers between devices with their start and end apart: 6 -> 0, of which waited for: 1 -> 0; matrix products, arithmetic and copies ran while one was open for 18% -> 0% of each run, Pallas kernels for 0% -> 0%
where the time goes in v1:
time: 239 us
  Pallas kernels  217 us (91%)
  local copies, waits for them, and re-layouts  19.4 us (8%)
    pallas_call x1, Pallas kernels, on_device(): pl.pallas_call(functools.partial(cluster_kernel, owners, share, capacity)...  213 us
    unnamed x15, local copies, waits for them, and re-layouts  17.7 us

profile of v1, /device:TPU:0, one launch (start us, length us, event | category | flops | bytes accessed | tf_op | source)
XLA Modules:
  0.0 239.0 jit_solution(7282546270141469731)
XLA Ops:
  0.6 0.7 dynamic_slice.3
  1.4 1.0 select_reduce_fusion.1
  2.4 0.7 multiply_add_fusion
  3.0 0.1 select_reduce_fusion
  3.2 0.1 sub.7.slots_ref
  3.2 0.1 select_n.23
  3.3 0.1 broadcast_in_dim.33.rate_ref
  3.4 0.0 copy-start
  3.4 2.2 copy-done
  5.6 0.0 copy-start.3
  5.6 4.5 %gather_pages.1 = (bf16[2,4096,128]{2,1,0:T(8,128)(2,1)S(1)}, bf16[4,2,12,128,128]{4,3,2,1,0:T(8,128)(2,1)S(1)}, bf16[4,2,12,128,128]{4,3,2,1,0:T(8,128)(2,1)S(1)}) custom-call(s32[192]{0:T(256)S(1)} %sub.7.slots_ref, s32[1]{0:T(128)} %bitcast.1.first_ref, f32[4,4096,128]{2,1,0:T(8,128)} %key_ref.1, bf16[4,4096,128]{2,1,0:T(8,128)(2,1)S(1)} %copy-done), custom_call_target="tpu_custom_call" | custom-call | tf_op jit(solution)/shard_map/gather_pages/pallas_call | solution.py:264
  10.1 0.0 copy-start.1
  10.2 1.7 copy-done.1
  11.8 0.0 copy-start.2
  11.8 1.7 copy-done.2
  13.5 0.0 copy-done.3
  13.5 212.6 %cluster_and_move.1 = (f32[4,256,128]{2,1,0:T(8,128)S(1)}, bf16[4,48,128,128]{3,2,1,0:T(8,128)(2,1)}, bf16[4,48,128,128]{3,2,1,0:T(8,128)(2,1)}, s32[4,8,128]{2,1,0:T(8,128)S(1)}) custom-call(bf16[2,4096,128]{2,1,0:T(8,128)(2,1)S(1)} %get-tuple-element.11.low_ref, f32[4,256,128]{2,1,0:T(8,128)S(1)} %copy-done.3, f32[2,8,128]{2,1,0:T(8,128)S(1)} %broadcast_in_dim.33.rate_ref, ...), custom_call_target="tpu_custom_call" | custom-call | tf_op jit(solution)/shard_map/cluster_and_move/pallas_call | solution.py:291
  226.1 0.7 reshape.51
  226.8 0.0 slice-start
  226.8 0.8 copy.18
  227.6 0.0 slice-start.1
  227.6 8.7 %copy.19 = bf16[4,48,128,128]{3,2,1,0:T(8,128)(2,1)} copy(bf16[4,48,128,128]{3,2,1,0:T(8,128)(2,1)} %get-tuple-element.25) | data formatting | bytes 12582912
  236.3 0.0 slice-done
  236.3 0.0 slice-done.1
  236.3 2.7 %copy.20 = bf16[4,48,128,128]{3,2,1,0:T(8,128)(2,1)} copy(bf16[4,48,128,128]{3,2,1,0:T(8,128)(2,1)S(1)} %bitcast.8) | data formatting | bytes 12582912
  (8 shorter events, 0.0 us)
Async XLA Ops:
  3.4 2.2 copy-start
  5.6 7.9 %copy-start.3 = (f32[4,256,128]{2,1,0:T(8,128)S(1)}, f32[4,256,128]{2,1,0:T(8,128)}, u32[]{:S(2)}) copy-start(f32[4,256,128]{2,1,0:T(8,128)} %cent_ref.1) | copy-start | bytes 1572868
  10.1 1.7 copy-start.1
  11.8 1.7 copy-start.2
  226.8 9.5 %slice-start = ((s8[6291456]{0:T(1024)(128)(4,1)}), s8[4194304]{0:T(1024)(128)(4,1)S(1)}, s32[]{:S(2)}) async-start(s8[6291456]{0:T(1024)(128)(4,1)} %bitcast.7), calls=%async_computation | async-start | bytes 8388608
  227.6 8.7 %slice-start.1 = ((s8[6291456]{0:T(1024)(128)(4,1)}), s8[2097152]{0:T(1024)(128)(4,1)S(1)}, s32[]{:S(2)}) async-start(s8[6291456]{0:T(1024)(128)(4,1)} %bitcast.7), calls=%async_computation.1 | async-start | bytes 4194304

commit v2 on v1

--- a/solution.py
+++ b/solution.py
@@ -63,14 +63,14 @@
 def cluster_kernel(owners, share, capacity, low_ref, cent_ref, rate_ref, ids_ref,
                    send_key_ref, send_value_ref,
                    clusters_ref, moved_key_ref, moved_value_ref, moved_ids_ref,
-                   keys_aug, table, table_aug, acc, part, part_in, mass, mass_in, total_rep,
-                   ids_in, fin,
-                   page_sems, fwd_sems, own_sems, own_fwd_sems, sum_sems, mass_sems, table_sems,
+                   keys_aug, keys_across, table, table_aug, acc, part, part_in, mass, mass_in, total_rep,
+                   norm_rep, norm, norm_in, low_table, ids_in, fin,
+                   page_sems, fwd_sems, own_sems, own_fwd_sems, sum_sems, mass_sems, table_sems, norm_sems,
                    ids_sems, cent_sems, fin_sems):
     me = lax.axis_index("seq")
     sub = lax.axis_index("sub")
     sib = 1 - sub
-    cents = table.shape[2]
+    cents = table.shape[1]
     half = cent_ref.shape[1]
     quarter = cents // owners
     tokens = low_ref.shape[1]
@@ -91,7 +91,7 @@
     waits = []
     first_head = sub * share
     cent_copy = remote(cent_ref.at[pl.ds(sib * share, share)],
-                       table.at[0, :, pl.ds(pl.multiple_of(sub * half, half), half), :],
+                       table.at[:, pl.ds(pl.multiple_of(sub * half, half), half), :],
                        cent_sems, (), {"sub": sib})
     cent_copy.start()
     ids_copies = []
@@ -147,7 +147,18 @@
     for h in range(share):
         keys_aug[h, :, :LANES] = low_ref[h]
         keys_aug[h, :, LANES:] = jnp.ones((tokens, LANES), jnp.bfloat16)
-        table[0, h, pl.ds(pl.multiple_of(sub * half, half), half), :] = cent_ref[first_head + h]
+        keys_across[h, LANES:, :] = jnp.ones((LANES, tokens), jnp.bfloat16)
+
+        def turn(i, carry, h=h):
+            cols = pl.ds(pl.multiple_of(i * TILE, TILE), TILE)
+            keys_across[h, :LANES, cols] = jnp.swapaxes(low_ref[h, cols, :], 0, 1)
+            return carry
+
+        lax.fori_loop(0, tokens // TILE, turn, 0)
+        table[h, pl.ds(pl.multiple_of(sub * half, half), half), :] = cent_ref[first_head + h]
+    norm_rep[...] = jnp.zeros(norm_rep.shape, jnp.float32)
+    norm[...] = jnp.zeros(norm.shape, jnp.float32)
+    mass[...] = jnp.zeros(mass.shape, jnp.float32)
     cent_copy.wait()
 
     lane = lax.broadcasted_iota(jnp.int32, (cents, LANES), 1)
@@ -156,29 +167,38 @@
     blocks = cents // LANES
     for it in range(ITERS):
         for h in range(share):
-            rows = table[it, h]
-            norm = jnp.broadcast_to(-0.5 * jnp.sum(rows * rows, axis=1, keepdims=True), rows.shape)
-            high = norm.astype(jnp.bfloat16).astype(jnp.float32)
-            rest = norm - high
+            if it == 0:
+                rows = table[h]
+                half_norm = jnp.broadcast_to(-0.5 * jnp.sum(rows * rows, axis=1, keepdims=True), rows.shape)
+                table_aug[h, :, :LANES] = rows.astype(jnp.bfloat16)
+            else:
+                for b in range(blocks):
+                    row = norms[h * blocks + b:h * blocks + b + 1, :]
+                    total_rep[b * LANES:(b + 1) * LANES, :] = jnp.broadcast_to(
+                        jnp.sum(jnp.where(eye, row, 0.0), axis=1, keepdims=True), (LANES, LANES))
+                half_norm = total_rep[...]
+                table_aug[h, :, :LANES] = low_table[it - 1, h]
+            high = half_norm.astype(jnp.bfloat16).astype(jnp.float32)
+            rest = half_norm - high
             mid = rest.astype(jnp.bfloat16).astype(jnp.float32)
             low = rest - mid
             extra = jnp.where(lane == 0, high, jnp.where(lane == 1, mid, jnp.where(lane == 2, low, 0.0)))
-            table_aug[h, :, :LANES] = rows.astype(jnp.bfloat16)
             table_aug[h, :, LANES:] = extra.astype(jnp.bfloat16)
             acc[h] = jnp.zeros((cents, 2 * LANES), jnp.float32)
-            rate = rate_ref[h, 0:1, 0:1] * (1.0 / math.log(2.0))
-
-            def sweep(i, carry, h=h, rate=rate):
-                k = keys_aug[h, pl.ds(pl.multiple_of(i * TILE, TILE), TILE), :]
-                s = lax.dot_general(table_aug[h], k, (((1,), (1,)), ((), ())),
-                                    preferred_element_type=jnp.float32)
+        rates = [rate_ref[h, 0:1, 0:1] * (1.0 / math.log(2.0)) for h in range(share)]
+
+        def sweep(i, carry, rates=rates):
+            cols = pl.ds(pl.multiple_of(i * TILE, TILE), TILE)
+            scores = [jnp.dot(table_aug[h], keys_across[h, :, cols],
+                              preferred_element_type=jnp.float32) for h in range(share)]
+            for h, s in enumerate(scores):
                 top = jnp.max(s, axis=0, keepdims=True)
-                p = jnp.exp2((s - top) * rate)
+                p = jnp.exp2((s - top) * rates[h])
                 w = (p * (1.0 / jnp.sum(p, axis=0, keepdims=True))).astype(jnp.bfloat16)
-                acc[h] += jnp.dot(w, k, preferred_element_type=jnp.float32)
-                return carry
-
-            lax.fori_loop(0, tokens // TILE, sweep, 0)
+                acc[h] += jnp.dot(w, keys_aug[h, cols, :], preferred_element_type=jnp.float32)
+            return carry
+
+        lax.fori_loop(0, tokens // TILE, sweep, 0)
         for h in range(share):
             part[it, h] = acc[h, :, :LANES].astype(jnp.bfloat16)
             for b in range(blocks):
@@ -208,27 +228,43 @@
             sums = acc[h, mine, :LANES]
             for i in range(owners - 1):
                 sums = sums + part_in[it, i, h].astype(jnp.float32)
-            table[it + 1, h, mine, :] = (sums + prior_count * table[it, h, mine, :]) / (
-                total_rep[mine, :] + prior_count)
+            fresh = (sums + prior_count * table[h, mine, :]) / (total_rep[mine, :] + prior_count)
+            table[h, mine, :] = fresh
+            low_table[it, h, mine, :] = fresh.astype(jnp.bfloat16)
+            if it + 1 < ITERS:
+                norm_rep[mine, :] = jnp.broadcast_to(
+                    -0.5 * jnp.sum(fresh * fresh, axis=1, keepdims=True), fresh.shape)
+                for b in range(blocks):
+                    norm[it, h * blocks + b:h * blocks + b + 1, :] = jnp.sum(
+                        jnp.where(eye, norm_rep[b * LANES:(b + 1) * LANES, :], 0.0), axis=0, keepdims=True)
         copies = []
         for i, q in enumerate(partners):
-            c = remote(table.at[it + 1, :, mine, :], table.at[it + 1, :, mine, :],
+            c = remote(low_table.at[it, :, mine, :], low_table.at[it, :, mine, :],
                        table_sems, (it, i), {"seq": q})
             c.start()
             copies.append(c)
+            if it + 1 < ITERS:
+                m = remote(norm.at[it], norm_in.at[it, i], norm_sems, (it, i), {"seq": q})
+                m.start()
+                copies.append(m)
         start_pages((4 + 2 * it) * step_pages)
         for c in copies:
             c.wait()
+        if it + 1 < ITERS:
+            norms = norm[it]
+            for i in range(owners - 1):
+                norms = norms + norm_in[it, i]
 
     start_pages(len(page_copies))
-    fin_copy = remote(table.at[ITERS, :, pl.ds(pl.multiple_of(sib * half, half), half), :], fin,
+    fin_copy = remote(low_table.at[ITERS - 1, :, pl.ds(pl.multiple_of(sib * half, half), half), :], fin,
                       fin_sems, (), {"sub": sib})
     fin_copy.start()
     for h in range(share):
-        clusters_ref[first_head + h] = table[ITERS, h, pl.ds(pl.multiple_of(sub * half, half), half), :]
+        clusters_ref[first_head + h] = low_table[
+            ITERS - 1, h, pl.ds(pl.multiple_of(sub * half, half), half), :].astype(jnp.float32)
     fin_copy.wait()
     for h in range(share):
-        clusters_ref[sib * share + h] = fin[h]
+        clusters_ref[sib * share + h] = fin[h].astype(jnp.float32)
     for c in ids_copies:
         c.wait()
     ids_in[me] = ids_ref[me]
@@ -298,7 +334,8 @@
         out_specs=[vmem, anyspace, anyspace, vmem],
         scratch_shapes=[
             pltpu.VMEM((share, tokens, 2 * LANES), jnp.bfloat16),
-            pltpu.VMEM((ITERS + 1, share, cents, width), jnp.float32),
+            pltpu.VMEM((share, 2 * LANES, tokens), jnp.bfloat16),
+            pltpu.VMEM((share, cents, width), jnp.float32),
             pltpu.VMEM((share, cents, 2 * LANES), jnp.bfloat16),
             pltpu.VMEM((share, cents, 2 * LANES), jnp.float32),
             pltpu.VMEM((ITERS, share, cents, width), jnp.bfloat16),
@@ -306,12 +343,17 @@
             pltpu.VMEM((ITERS, 8, LANES), jnp.float32),
             pltpu.VMEM((ITERS, rest, 8, LANES), jnp.float32),
             pltpu.VMEM((cents, LANES), jnp.float32),
+            pltpu.VMEM((cents, LANES), jnp.float32),
+            pltpu.VMEM((ITERS, 8, LANES), jnp.float32),
+            pltpu.VMEM((ITERS, rest, 8, LANES), jnp.float32),
+            pltpu.VMEM((ITERS, share, cents, width), jnp.bfloat16),
             pltpu.VMEM((owners, 8, LANES), jnp.int32),
-            pltpu.VMEM((share, half, width), jnp.float32),
+            pltpu.VMEM((share, half, width), jnp.bfloat16),
             dma((2, rest, 2, share)),
             dma((2, rest, 2, share)),
             dma((2, share)),
             dma((2, 2, share)),
+            dma((2, ITERS, rest)),
             dma((2, ITERS, rest)),
             dma((2, ITERS, rest)),
             dma((2, ITERS, rest)),
@@ -320,7 +362,7 @@
             dma((2,)),
         ],
         compiler_params=pltpu.CompilerParams(
-            collective_id=0, has_side_effects=True, vmem_limit_bytes=48 * 2**20),
+            collective_id=0, has_side_effects=True, vmem_limit_bytes=40 * 2**20),
         name="cluster_and_move",
     )(keys_low, centroids, rates, ids, send_keys, send_values)
     moved_ids = jnp.transpose(moved_ids[:, :heads, :capacity], (1, 0, 2)).reshape(heads, owners * capacity)

time: 239 us -> 220 us (0.921)
  Pallas kernels: 217 us -> 201 us
  local copies, waits for them, and re-layouts: 19.4 us -> 16.1 us
    pallas_call x1, Pallas kernels: 213 us -> 197 us  [on_device(): pl.pallas_call(functools.partial(cluster_kernel, owners, share, capacity)...]
    unnamed x15 -> x11, local copies, waits for them, and re-layouts: 17.7 us -> 14.4 us
where the time goes in v2:
time: 220 us
  Pallas kernels  201 us (91%)
  local copies, waits for them, and re-layouts  16.1 us (7%)
    pallas_call x1, Pallas kernels, on_device(): pl.pallas_call(functools.partial(cluster_kernel, owners, share, capacity)...  197 us
    unnamed x11, local copies, waits for them, and re-layouts  14.4 us
    pallas_call x1, Pallas kernels, on_device(): pl.pallas_call(functools.partial(gather_kernel, share, owners, capacity),...  4.53 us

profile of v2, /device:TPU:0, one launch (start us, length us, event | category | flops | bytes accessed | tf_op | source)
XLA Modules:
  0.0 219.7 jit_solution(7650837662455822694)
XLA Ops:
  0.6 0.7 dynamic_slice.3
  1.4 1.0 select_reduce_fusion.1
  2.4 0.7 multiply_add_fusion
  3.0 0.1 select_reduce_fusion
  3.2 0.1 sub.7.slots_ref
  3.2 0.1 select_n.23
  3.3 0.1 broadcast_in_dim.33.rate_ref
  3.4 0.0 copy-start
  3.4 2.2 copy-done
  5.6 0.0 copy-start.1
  5.6 4.5 %gather_pages.1 = (bf16[2,4096,128]{2,1,0:T(8,128)(2,1)S(1)}, bf16[4,2,12,128,128]{4,3,2,1,0:T(8,128)(2,1)S(1)}, bf16[4,2,12,128,128]{4,3,2,1,0:T(8,128)(2,1)S(1)}) custom-call(s32[192]{0:T(256)S(1)} %sub.7.slots_ref, s32[1]{0:T(128)} %bitcast.1.first_ref, f32[4,4096,128]{2,1,0:T(8,128)} %key_ref.1, bf16[4,4096,128]{2,1,0:T(8,128)(2,1)S(1)} %copy-done), custom_call_target="tpu_custom_call" | custom-call | tf_op jit(solution)/shard_map/gather_pages/pallas_call | solution.py:300
  10.1 0.0 copy-done.1
  10.2 196.6 %cluster_and_move.1 = (f32[4,256,128]{2,1,0:T(8,128)S(1)}, bf16[4,48,128,128]{3,2,1,0:T(8,128)(2,1)}, bf16[4,48,128,128]{3,2,1,0:T(8,128)(2,1)}, s32[4,8,128]{2,1,0:T(8,128)S(1)}) custom-call(bf16[2,4096,128]{2,1,0:T(8,128)(2,1)S(1)} %get-tuple-element.11.low_ref, f32[4,256,128]{2,1,0:T(8,128)S(1)} %copy-done.1, f32[2,8,128]{2,1,0:T(8,128)S(1)} %broadcast_in_dim.33.rate_ref, ...), custom_call_target="tpu_custom_call" | custom-call | tf_op jit(solution)/shard_map/cluster_and_move/pallas_call | solution.py:327
  206.8 0.7 reshape.51
  207.4 0.0 slice-start
  207.4 0.8 copy.18
  208.2 0.0 slice-start.1
  208.2 8.7 %copy.19 = bf16[4,48,128,128]{3,2,1,0:T(8,128)(2,1)} copy(bf16[4,48,128,128]{3,2,1,0:T(8,128)(2,1)} %get-tuple-element.25) | data formatting | bytes 12582912
  216.9 0.0 slice-done
  216.9 0.0 slice-done.1
  217.0 2.7 %copy.20 = bf16[4,48,128,128]{3,2,1,0:T(8,128)(2,1)} copy(bf16[4,48,128,128]{3,2,1,0:T(8,128)(2,1)S(1)} %bitcast.8) | data formatting | bytes 12582912
  (8 shorter events, 0.0 us)
Async XLA Ops:
  3.4 2.2 copy-start
  5.6 4.5 %copy-start.1 = (f32[4,256,128]{2,1,0:T(8,128)S(1)}, f32[4,256,128]{2,1,0:T(8,128)}, u32[]{:S(2)}) copy-start(f32[4,256,128]{2,1,0:T(8,128)} %cent_ref.1) | copy-start | bytes 1572868
  207.4 9.5 %slice-start = ((s8[6291456]{0:T(1024)(128)(4,1)}), s8[4194304]{0:T(1024)(128)(4,1)S(1)}, s32[]{:S(2)}) async-start(s8[6291456]{0:T(1024)(128)(4,1)} %bitcast.7), calls=%async_computation | async-start | bytes 8388608
  208.2 8.7 %slice-start.1 = ((s8[6291456]{0:T(1024)(128)(4,1)}), s8[2097152]{0:T(1024)(128)(4,1)S(1)}, s32[]{:S(2)}) async-start(s8[6291456]{0:T(1024)(128)(4,1)} %bitcast.7), calls=%async_computation.1 | async-start | bytes 4194304
